TPU v7x, 256 devices: a whole 4x4x8 slice. The times are simulated.
256 devices in a mesh: batch: 32 (over x, z), node: 4 (over y), replica: 2 (over core).
Axes of the slice: x: 4, y: 4, z: 8, core: 2. Of those that a mesh axis runs over, the one named last changes fastest.
Arguments:
- embed_table: bfloat16 [32768, 1024], P('batch'), may hold values from -6 to 6
- owner_shard: int32 [64, 256, 1], P(('batch', 'replica')), may hold values from 0 to 31; in each aligned block of 256 rows (0 to 255, 256 to 511, ..., all dimensions but the last counted through in order) at most 12 rows name the same one
- local_row: int32 [64, 256], P(('batch', 'replica')), may hold values from 0 to 1023
- lengths: int32 [64], P(('batch', 'replica')), may hold values from 64 to 256
- spd_bucket: int32 [64, 256, 256], P(('batch', 'replica')), may hold values from 0 to 15, as said below
- degree_bucket: int32 [64, 256], P(('batch', 'replica')), may hold values from 0 to 31, as said below
- w_query: bfloat16 [1024, 1024], P(None, 'node'), may hold values from -0.1875 to 0.1875
- w_key: bfloat16 [1024, 1024], P(None, 'node'), may hold values from -0.1875 to 0.1875
- w_value: bfloat16 [1024, 1024], P(None, 'node'), may hold values from -0.1875 to 0.1875
- w_out: bfloat16 [1024, 1024], P('node'), may hold values from -0.1875 to 0.1875
- spd_bias: float32 [16, 16], P(None, 'node'), may hold values from -4 to 4
- degree_bias: float32 [32, 16], P(None, 'node'), may hold values from -2 to 253
- cotangent: bfloat16 [64, 256, 1024], P(('batch', 'replica')), may hold values from -6 to 6
Outputs:
- table_grad: float32 [32768, 1024], P('batch', ('node', 'replica'))
- query_grad: float32 [1024, 1024], P(None, 'node')
- key_grad: float32 [1024, 1024], P(None, 'node')
- value_grad: float32 [1024, 1024], P(None, 'node')
- out_grad: float32 [1024, 1024], P('node')
- spd_grad: float32 [16, 16], P(None, 'node')
- degree_grad: float32 [32, 16], P(None, 'node')
Inputs may be any that keep to these rules, and one draw needn't show every extreme that they name: `owner_shard`: in each aligned block of 256 slots (the subgraphs of one index of batch and replica) no owner shard is named by more than 12 slots, a bound that some block reaches. `lengths`: slots at or past a subgraph's length are padding. `spd_bucket`: symmetric in its last two dimensions, 0 exactly on the diagonal. `degree_bucket`: some subgraphs hold only buckets below half of 32.
All inputs are finite; a program needn't handle non-finite values.
Results may differ from a plain program's by a relative error of at most 0.015.
Values may be sent and summed in bfloat16 or wider, within the bound.
A program may use at most 64 MiB of HBM per device.

v0:
```python
import jax
import jax.numpy as jnp
from jax import lax
from jax.sharding import PartitionSpec as P

HEAD_DIM = 64
NSPD = 16
NDEG = 32
EPS = 1e-05


def normalize(rows_in):
    widened = rows_in.astype(jnp.float32)
    mean_val = jnp.mean(widened, axis=-1, keepdims=True)
    centred = widened - mean_val
    inv_std = lax.rsqrt(jnp.mean(centred * centred, axis=-1, keepdims=True) + EPS)
    return (centred * inv_std, inv_std)


def on_device(
    embed_table,
    owner_shard,
    local_row,
    lengths,
    spd_bucket,
    degree_bucket,
    w_query,
    w_key,
    w_value,
    w_out,
    spd_bias,
    degree_bias,
    cotangent,
):
    group_count, slot_count, feature_dim = cotangent.shape
    slot_total = group_count * slot_count
    row_count = embed_table.shape[0]
    peer_count = lax.axis_size("batch")
    capacity = 3 * slot_total // (2 * peer_count)
    dest_shard = owner_shard.reshape(slot_total)
    wanted = local_row.reshape(slot_total)
    bucket_hits = (dest_shard[:, None] == jnp.arange(peer_count, dtype=jnp.int32)[None, :]).astype(
        jnp.int32
    )
    bucket_rank = jnp.sum((jnp.cumsum(bucket_hits, axis=0) - bucket_hits) * bucket_hits, axis=1)
    slot_place = dest_shard * capacity + bucket_rank
    requests = jnp.full((peer_count * capacity,), -1, jnp.int32).at[slot_place].set(wanted)
    asked_rows = lax.all_to_all(
        requests.reshape(peer_count, capacity), "batch", split_axis=0, concat_axis=0, tiled=True
    ).reshape(peer_count * capacity)
    present = asked_rows >= 0
    safe_rows = jnp.where(present, asked_rows, 0)
    target_rows = jnp.where(present, asked_rows, row_count)
    fetched = lax.all_to_all(
        embed_table[safe_rows].reshape(peer_count, capacity, feature_dim),
        "batch",
        split_axis=0,
        concat_axis=0,
        tiled=True,
    )
    slot_rows = fetched.reshape(peer_count * capacity, feature_dim)[slot_place]
    x_hat, inv_std = normalize(slot_rows)
    normed = x_hat.astype(jnp.bfloat16)
    local_width = w_query.shape[1]
    head_local = local_width // HEAD_DIM
    head_shape = (group_count, slot_count, head_local, HEAD_DIM)
    score_scale = HEAD_DIM ** (-0.5)

    def project(weight):
        return jnp.dot(normed, weight, preferred_element_type=jnp.float32).astype(jnp.bfloat16)

    queries = project(w_query).reshape(head_shape)
    key_rows = project(w_key).reshape(head_shape)
    values = project(w_value).reshape(head_shape)
    valid_slot = jnp.arange(slot_count, dtype=jnp.int32)[None, :] < lengths[:, None]
    spd_hot = (spd_bucket[..., None] == jnp.arange(NSPD, dtype=jnp.int32)).astype(jnp.float32)
    degree_hot = (degree_bucket[..., None] == jnp.arange(NDEG, dtype=jnp.int32)).astype(jnp.float32)
    spd_term = jnp.einsum("gijb,bh->ghij", spd_hot, spd_bias, precision=lax.Precision.HIGHEST)
    degree_term = jnp.einsum(
        "gjb,bh->ghj", degree_hot, degree_bias, precision=lax.Precision.HIGHEST
    )[:, :, None, :]
    scores = (
        jnp.einsum("gihd,gjhd->ghij", queries, key_rows, preferred_element_type=jnp.float32)
        * score_scale
        + spd_term
        + degree_term
    )
    scores = jnp.where(valid_slot[:, None, None, :], scores, -jnp.inf)
    row_top = jnp.max(scores, axis=-1, keepdims=True)
    exp_scores = jnp.exp(scores - row_top)
    probs = exp_scores / jnp.sum(exp_scores, axis=-1, keepdims=True)
    probs_b = probs.astype(jnp.bfloat16)
    attended = (
        jnp.einsum("ghij,gjhd->gihd", probs_b, values, preferred_element_type=jnp.float32)
        .astype(jnp.bfloat16)
        .reshape(slot_total, local_width)
    )
    d_masked = jnp.where(valid_slot[:, :, None], cotangent, jnp.zeros_like(cotangent)).reshape(
        slot_total, feature_dim
    )
    d_att = jnp.dot(d_masked, w_out.T, preferred_element_type=jnp.float32).astype(jnp.bfloat16)
    out_part = jnp.dot(attended.T, d_masked, preferred_element_type=jnp.float32)
    d_att_h = d_att.reshape(head_shape)
    d_values = (
        jnp.einsum("ghij,gihd->gjhd", probs_b, d_att_h, preferred_element_type=jnp.float32)
        .astype(jnp.bfloat16)
        .reshape(slot_total, local_width)
    )
    d_probs = jnp.einsum("gihd,gjhd->ghij", d_att_h, values, preferred_element_type=jnp.float32)
    d_scores = probs * (d_probs - jnp.sum(probs * d_probs, axis=-1, keepdims=True))
    spd_part = jnp.einsum("gijb,ghij->bh", spd_hot, d_scores, precision=lax.Precision.HIGHEST)
    degree_part = jnp.einsum("gjb,ghij->bh", degree_hot, d_scores, precision=lax.Precision.HIGHEST)
    d_scores_b = d_scores.astype(jnp.bfloat16)
    d_queries = (
        (
            jnp.einsum("ghij,gjhd->gihd", d_scores_b, key_rows, preferred_element_type=jnp.float32)
            * score_scale
        )
        .astype(jnp.bfloat16)
        .reshape(slot_total, local_width)
    )
    d_keys = (
        (
            jnp.einsum("ghij,gihd->gjhd", d_scores_b, queries, preferred_element_type=jnp.float32)
            * score_scale
        )
        .astype(jnp.bfloat16)
        .reshape(slot_total, local_width)
    )
    query_part = jnp.dot(normed.T, d_queries, preferred_element_type=jnp.float32)
    key_part = jnp.dot(normed.T, d_keys, preferred_element_type=jnp.float32)
    value_part = jnp.dot(normed.T, d_values, preferred_element_type=jnp.float32)
    d_normed = (
        jnp.dot(d_queries, w_query.T, preferred_element_type=jnp.float32)
        + jnp.dot(d_keys, w_key.T, preferred_element_type=jnp.float32)
        + jnp.dot(d_values, w_value.T, preferred_element_type=jnp.float32)
    )
    lead_flag = (lax.axis_index("node") == 0).astype(jnp.float32)
    d_rows = lead_flag * d_masked.astype(jnp.float32) + inv_std * (
        d_normed
        - jnp.mean(d_normed, axis=-1, keepdims=True)
        - x_hat * jnp.mean(d_normed * x_hat, axis=-1, keepdims=True)
    )
    send_back = (
        jnp.zeros((peer_count * capacity, feature_dim), jnp.float32).at[slot_place].set(d_rows)
    )
    returned = (
        lax.all_to_all(
            send_back.reshape(peer_count, capacity, feature_dim).astype(jnp.bfloat16),
            "batch",
            split_axis=0,
            concat_axis=0,
            tiled=True,
        )
        .astype(jnp.float32)
        .reshape(peer_count * capacity, feature_dim)
    )
    accum = (
        jnp.zeros((row_count, feature_dim), jnp.float32).at[target_rows].add(returned, mode="drop")
    )
    table_grad = lax.psum_scatter(
        accum.astype(jnp.bfloat16), ("node", "replica"), scatter_dimension=1, tiled=True
    ).astype(jnp.float32)
    summed = lax.psum(
        (query_part, key_part, value_part, out_part, spd_part, degree_part), ("batch", "replica")
    )
    copies = float(peer_count * lax.axis_size("replica"))
    return (
        table_grad,
        summed[0] / copies,
        summed[1] / copies,
        summed[2] / copies,
        summed[3] / copies,
        summed[4] / copies,
        summed[5] / copies,
    )


def solution(mesh):
    placed = (
        P("batch", None),
        P(("batch", "replica"), None, None),
        P(("batch", "replica"), None),
        P(("batch", "replica")),
        P(("batch", "replica"), None, None),
        P(("batch", "replica"), None),
        P(None, "node"),
        P(None, "node"),
        P(None, "node"),
        P("node", None),
        P(None, "node"),
        P(None, "node"),
        P(("batch", "replica"), None, None),
    )
    return jax.shard_map(
        on_device,
        mesh=mesh,
        in_specs=placed,
        out_specs=(
            P("batch", ("node", "replica")),
            P(None, "node"),
            P(None, "node"),
            P(None, "node"),
            P("node", None),
            P(None, "node"),
            P(None, "node"),
        ),
        check_vma=False,
    )
```

profile of v0, /device:TPU:8, one launch (start us, length us, event | category | flops | bytes accessed | tf_op | source)
XLA Modules:
  0.0 310.1 jit_solution(10417535351380792851)
XLA Ops:
  11.1 1.6 scatter_custom_fusion
  12.8 20.9 %all_to_all.19 = s32[32,1,12]{2,1,0:T(1,128)S(1)} all-to-all(s32[32,1,12]{2,1,0:T(1,128)S(1)} %bitcast.120), channel_id=1, replica_groups=mesh['batch'=32,'node'=4,'replica'=2] {'batch'}, dimensions={0} | all-to-all | bytes 3072 | tf_op jit(solution)/shard_map/all_to_all | solution.py:48
  35.6 2.1 gather_fusion
  38.9 4.7 %all-to-all-start.1 = ((bf16[32,12,1024]{2,1,0:T(8,128)(2,1)}), bf16[32,12,1024]{2,1,0:T(8,128)(2,1)}, u32[]{:S(2)}, u32[]{:S(2)}) async-start(bf16[32,12,1024]{2,1,0:T(8,128)(2,1)} %reshape.327), calls=%async_computation.1 | async-start | bytes 2097152 | tf_op jit(solution)/shard_map/all_to_all | solution.py:54
  43.6 1.3 fusion.2
  44.9 1.4 copy.39
  47.2 2.3 convolution_convert_fusion.3
  49.5 21.5 %all-to-all-done.1 = bf16[32,12,1024]{2,1,0:T(8,128)(2,1)} async-done(((bf16[32,12,1024]{2,1,0:T(8,128)(2,1)}), bf16[32,12,1024]{2,1,0:T(8,128)(2,1)}, u32[]{:S(2)}, u32[]{:S(2)}) %all-to-all-start.1) | async-done | bytes 786464 | tf_op jit(solution)/shard_map/all_to_all | solution.py:54
  71.1 1.3 reshape.328
  74.0 1.5 convolution_convert_fusion.5
  79.5 1.9 convolution_convert_fusion.1
  81.5 2.4 fusion.68
  83.9 1.4 fusion.60
  85.3 1.9 convolution_convert_fusion
  87.3 1.5 fusion.58
  88.7 1.5 fusion.56
  90.2 1.4 fusion.31
  91.8 1.8 convolution_add_fusion.1
  93.6 1.4 fusion.65
  95.0 3.8 %scatter_custom_fusion.1 = f32[384,1024]{1,0:T(8,128)} fusion(s32[256]{0:T(256)} %bitcast.125, bf16[256,1024]{1,0:T(8,128)(2,1)S(1)} %gather_fusion.1, f32[256,1024]{1,0:T(8,128)} %get-tuple-element.23, f32[]{:T(128)} %constant.15.clone.1, f32[256]{0:T(256)S(1)} %get-tuple-element.24, f32[256]{0:T(256)S(1)} %get-tuple-element.25, ...), kind=kCustom, calls=%fused_computation.44 | custom fusion | flops 2883584 | bytes 3674884 | tf_op jit(solution)/shard_map/scatter | solution.py:145
  98.8 2.5 convert_element_type.111
  102.5 35.3 %all_to_all.20 = bf16[32,12,1024]{2,1,0:T(8,128)(2,1)} all-to-all(bf16[32,12,1024]{2,1,0:T(8,128)(2,1)S(1)} %convert_element_type.112), channel_id=1, replica_groups=mesh['batch'=32,'node'=4,'replica'=2] {'batch'}, dimensions={0} | all-to-all | bytes 1572864 | tf_op jit(solution)/shard_map/all_to_all | solution.py:148
  137.9 2.4 reshape.377
  140.2 6.6 %scatter_custom_fusion.2 = f32[1024,1024]{1,0:T(8,128)} fusion(s32[384]{0:T(512)} %get-tuple-element.10, f32[384,1024]{1,0:T(8,128)} %reshape.377, f32[]{:T(128)} %constant.15.clone.1), kind=kCustom, calls=%fused_computation.11 | custom fusion | flops 393216 | bytes 4194816 | tf_op jit(solution)/shard_map/scatter-add | solution.py:159
  146.9 3.9 %convert_element_type.113 = bf16[1024,1024]{1,0:T(8,128)(2,1)} convert(f32[1024,1024]{1,0:T(8,128)} %scatter_custom_fusion.2) | non-fusion elementwise | flops 1048576 | bytes 6291456 | tf_op jit(solution)/shard_map/convert_element_type | solution.py:162
  150.8 4.0 %copy.52 = bf16[1024,1024]{0,1:T(8,128)(2,1)} copy(bf16[1024,1024]{1,0:T(8,128)(2,1)} %convert_element_type.113) | data formatting | bytes 4194304
  156.0 1.3 copy.46
  157.3 4.0 %fusion.19 = f32[16,4]{0,1:T(4,128)S(1)} fusion(f32[4,256,256]{2,0,1:T(4,128)} %copy.46, s32[256,256]{1,0:T(8,128)S(1)} %bitcast.117), kind=kOutput, calls=%fused_computation.39 | convolution fusion | flops 51380224 | bytes 1310976 | tf_op jit(solution)/shard_map/gijb,ghij->bh/dot_general | solution.py:111
  161.5 127.4 %all-reduce = (f32[16,4]{0,1:T(4,128)S(1)}, f32[32,4]{0,1:T(4,128)S(1)}) all-reduce(f32[16,4]{0,1:T(4,128)S(1)} %fusion.19, f32[32,4]{0,1:T(4,128)S(1)} %fusion.44), channel_id=1, replica_groups=mesh['batch'=32,'node'=4,'replica'=2] {'batch','replica'}, use_global_device_ids=true, to_apply=%region_18.19 | all-reduce | flops 192 | bytes 1536 | tf_op jit(solution)/shard_map/psum | solution.py:164
  290.0 5.7 %all-reduce.4.cloned.1.call-done = (f32[1024,256]{1,0:T(8,128)}, f32[1024,256]{1,0:T(8,128)}, f32[1024,256]{1,0:T(8,128)}, f32[256,1024]{1,0:T(8,128)}) async-done(((f32[1024,256]{1,0:T(8,128)}, f32[1024,256]{1,0:T(8,128)}, f32[1024,256]{1,0:T(8,128)}, f32[256,1024]{1,0:T(8,128)}), (f32[1024,256]{1,0:T(8,128)}, f32[1024,256]{1,0:T(8,128)}, f32[1024,256]{1,0:T(8,128)}, ...) | async-done | bytes 4194320 | tf_op jit(solution)/shard_map/psum | solution.py:164
  295.7 2.4 broadcast_multiply_fusion.3
  299.2 1.5 broadcast_multiply_fusion.1
  (83 shorter events, 19.3 us)
Async XLA Ops:
  8.0 27.6 %copy-start = (bf16[1024,1024]{1,0:T(8,128)(2,1)S(1)}, bf16[1024,1024]{1,0:T(8,128)(2,1)}, u32[]{:S(2)}) copy-start(bf16[1024,1024]{1,0:T(8,128)(2,1)} %param.13) | copy-start | bytes 6291460
  11.1 35.8 %copy-start.14 = (s32[256,1]{0,1:T(1,128)}, s32[256,1]{0,1:T(1,128)S(1)}, u32[]{:S(2)}) copy-start(s32[256,1]{0,1:T(1,128)S(1)} %compare_select_fusion.4) | copy-start | bytes 3076
  37.7 5.9 %copy-start.12 = (s32[1,256,256]{2,1,0:T(8,128)S(1)}, s32[1,256,256]{2,1,0:T(8,128)}, u32[]{:S(2)}) copy-start(s32[1,256,256]{2,1,0:T(8,128)} %param.17) | copy-start | bytes 786436
  37.7 5.9 %copy-start.15 = (f32[16,4]{0,1:T(4,128)S(1)}, f32[16,4]{0,1:T(4,128)}, u32[]{:S(2)}) copy-start(f32[16,4]{0,1:T(4,128)} %param.23) | copy-start | bytes 772
  38.9 32.2 %all-to-all-start.1 = ((bf16[32,12,1024]{2,1,0:T(8,128)(2,1)}), bf16[32,12,1024]{2,1,0:T(8,128)(2,1)}, u32[]{:S(2)}, u32[]{:S(2)}) async-start(bf16[32,12,1024]{2,1,0:T(8,128)(2,1)} %reshape.327), calls=%async_computation.1 | async-start | bytes 2097152 | tf_op jit(solution)/shard_map/all_to_all | solution.py:54
  43.5 3.4 %copy-start.16 = (f32[32,4]{0,1:T(4,128)S(1)}, f32[32,4]{0,1:T(4,128)}, u32[]{:S(2)}) copy-start(f32[32,4]{0,1:T(4,128)} %param.24) | copy-start | bytes 1540
  43.5 3.4 %copy-start.17 = (s32[1,256]{1,0:T(1,128)S(1)}, s32[1,256]{1,0:T(1,128)}, u32[]{:S(2)}) copy-start(s32[1,256]{1,0:T(1,128)} %param.18) | copy-start | bytes 3076
  43.5 252.2 %all-reduce.4.cloned.1.call-start = ((), (), s32[]{:S(2)}) async-start(), calls=%async_computation.5 | async-start | bytes 8388608 | tf_op jit(solution)/shard_map/psum | solution.py:164
  73.6 2.0 copy-start.11
  73.6 2.4 copy-start.3
  76.0 1.2 copy-start.9
  76.4 1.6 copy-start.4
  76.4 1.3 copy-start.19
  78.3 1.0 copy-start.1
  87.3 2.9 copy-start.5
  91.6 209.1 %reduce-scatter.4.cloned.1.call-start = ((), (), s32[]{:S(2)}) async-start(), calls=%async_computation.4 | async-start | bytes 2359296
  91.8 1.8 copy-start.10
  154.7 1.2 copy-start.2
  154.7 2.5 copy-start.13
  156.0 5.3 %copy-start.18 = (s32[1,256]{1,0:T(1,128)S(1)}, s32[1,256]{1,0:T(1,128)}, u32[]{:S(2)}) copy-start(s32[1,256]{1,0:T(1,128)} %param.18) | copy-start | bytes 3076
  295.7 2.4 copy-start.6
  295.7 3.5 %copy-start.7 = (f32[1024,256]{1,0:T(8,128)S(1)}, f32[1024,256]{1,0:T(8,128)}, u32[]{:S(2)}) copy-start(f32[1024,256]{1,0:T(8,128)} %get-tuple-element.14) | copy-start | bytes 3145732
  295.7 3.5 %copy-start.8 = (f32[1024,256]{1,0:T(8,128)S(1)}, f32[1024,256]{1,0:T(8,128)}, u32[]{:S(2)}) copy-start(f32[1024,256]{1,0:T(8,128)} %get-tuple-element.15) | copy-start | bytes 3145732
Sparse Core Ops, SparseCore 0:
  91.7 203.9 all-reduce.3
Sparse Core Ops, SparseCore 1:
  154.8 32.6 reduce-scatter.3
where the time goes:
time: 311 us; the launch traced here: 310 us
  blocking collectives  184 us (59%)
  other arithmetic  29.4 us (9%)
  waiting for transfers between devices  27.2 us (9%)
  matrix products  26.8 us (9%)
  local copies, waits for them, and re-layouts  21.6 us (7%)
  between operations  16.5 us (5%)
  starting transfers between devices  4.93 us (2%)
    psum x1, blocking collectives, on_device(): lax.psum((query_part, key_part, value_part, out_part, spd_part, degree_pa...  127 us
    all_to_all x1, blocking collectives, on_device(): lax.all_to_all(send_back.reshape(peer_count, capacity, feature_dim).astyp...  35.3 us
    all_to_all x1, waiting for transfers between devices, on_device(): lax.all_to_all(embed_table[safe_rows].reshape(peer_count, capacity, featu...  21.5 us
    all_to_all x1, blocking collectives, on_device(): lax.all_to_all(requests.reshape(peer_count, capacity), 'batch', split_axi...  20.9 us
    unnamed x42, local copies, waits for them, and re-layouts  7.15 us
    scatter-add x1, other arithmetic, on_device(): jnp.zeros((row_count, feature_dim), jnp.float32).at[target_rows]  6.64 us
  transfers between devices with their start and end apart: 3, of which 2 were waited for; matrix products, arithmetic and copies ran while one was open for 14% of the time, Pallas kernels for 0%

commit v1 on v0

--- a/solution.py
+++ b/solution.py
@@ -161,9 +161,9 @@
     table_grad = lax.psum_scatter(
         accum.astype(jnp.bfloat16), ("node", "replica"), scatter_dimension=1, tiled=True
     ).astype(jnp.float32)
-    summed = lax.psum(
-        (query_part, key_part, value_part, out_part, spd_part, degree_part), ("batch", "replica")
-    )
+    summed = (query_part, key_part, value_part, out_part, spd_part, degree_part)
+    for kk in ("replica", "batch"):
+        summed = lax.psum(summed, kk)
     copies = float(peer_count * lax.axis_size("replica"))
     return (
         table_grad,

time: 311 us -> 332 us (1.068)
  waiting for transfers between devices: 27.2 us -> 105 us
  blocking collectives: 184 us -> 128 us
    psum x1 -> x2, waiting for transfers between devices: 5.65 us -> 82.4 us  [on_device(): summed = lax.psum(summed, kk)]
    psum x1 -> x2, blocking collectives: 127 us -> 74.6 us  [on_device(): summed = lax.psum(summed, kk)]
    unnamed x42 -> x48, local copies, waits for them, and re-layouts: 7.15 us -> 6.51 us
  transfers between devices with their start and end apart: 3 -> 4, of which waited for: 2 -> 2; matrix products, arithmetic and copies ran while one was open for 14% -> 13% of each run, Pallas kernels for 0% -> 0%
where the time goes in v1:
time: 332 us; the launch traced here: 331 us
  blocking collectives  128 us (39%)
  waiting for transfers between devices  105 us (32%)
  other arithmetic  29.3 us (9%)
  matrix products  26.5 us (8%)
  local copies, waits for them, and re-layouts  21.1 us (6%)
  between operations  16.5 us (5%)
  starting transfers between devices  4.97 us (1%)
    psum x2, waiting for transfers between devices, on_device(): summed = lax.psum(summed, kk)  82.4 us
    psum x2, blocking collectives, on_device(): summed = lax.psum(summed, kk)  74.6 us
    all_to_all x1, blocking collectives, on_device(): lax.all_to_all(send_back.reshape(peer_count, capacity, feature_dim).astyp...  32.3 us
    all_to_all x1, waiting for transfers between devices, on_device(): lax.all_to_all(embed_table[safe_rows].reshape(peer_count, capacity, featu...  21.6 us
    all_to_all x1, blocking collectives, on_device(): lax.all_to_all(requests.reshape(peer_count, capacity), 'batch', split_axi...  20.9 us
    scatter-add x1, other arithmetic, on_device(): jnp.zeros((row_count, feature_dim), jnp.float32).at[target_rows]  6.64 us
  transfers between devices with their start and end apart: 4, of which 2 were waited for; matrix products, arithmetic and copies ran while one was open for 13% of the time, Pallas kernels for 0%

profile of v1, /device:TPU:8, one launch (start us, length us, event | category | flops | bytes accessed | tf_op | source)
XLA Modules:
  0.0 330.8 jit_solution(12936966542751065852)
XLA Ops:
  11.1 1.6 scatter_custom_fusion
  12.8 20.9 %all_to_all.19 = s32[32,1,12]{2,1,0:T(1,128)S(1)} all-to-all(s32[32,1,12]{2,1,0:T(1,128)S(1)} %bitcast.120), channel_id=1, replica_groups=mesh['batch'=32,'node'=4,'replica'=2] {'batch'}, dimensions={0} | all-to-all | bytes 3072 | tf_op jit(solution)/shard_map/all_to_all | solution.py:48
  35.6 2.1 gather_fusion
  38.9 4.7 %all-to-all-start.1 = ((bf16[32,12,1024]{2,1,0:T(8,128)(2,1)}), bf16[32,12,1024]{2,1,0:T(8,128)(2,1)}, u32[]{:S(2)}, u32[]{:S(2)}) async-start(bf16[32,12,1024]{2,1,0:T(8,128)(2,1)} %reshape.327), calls=%async_computation.1 | async-start | bytes 2097152 | tf_op jit(solution)/shard_map/all_to_all | solution.py:54
  44.9 1.4 copy.39
  47.2 2.3 convolution_convert_fusion.3
  49.5 21.6 %all-to-all-done.1 = bf16[32,12,1024]{2,1,0:T(8,128)(2,1)} async-done(((bf16[32,12,1024]{2,1,0:T(8,128)(2,1)}), bf16[32,12,1024]{2,1,0:T(8,128)(2,1)}, u32[]{:S(2)}, u32[]{:S(2)}) %all-to-all-start.1) | async-done | bytes 786464 | tf_op jit(solution)/shard_map/all_to_all | solution.py:54
  71.1 1.3 reshape.328
  74.0 1.5 convolution_convert_fusion.5
  79.6 2.1 convolution_convert_fusion.1
  81.7 2.8 convolution_convert_fusion
  84.5 1.4 fusion.60
  85.9 1.5 fusion.58
  87.4 1.4 fusion.56
  88.8 1.3 fusion.31
  90.5 1.4 fusion.68
  91.9 1.4 convolution_add_fusion.1
  93.3 1.4 fusion.65
  94.8 3.8 %scatter_custom_fusion.1 = f32[384,1024]{1,0:T(8,128)} fusion(s32[256]{0:T(256)} %bitcast.125, bf16[256,1024]{1,0:T(8,128)(2,1)S(1)} %gather_fusion.1, f32[256,1024]{1,0:T(8,128)} %get-tuple-element.29, f32[]{:T(128)} %constant.15.clone.1, f32[256]{0:T(256)S(1)} %get-tuple-element.30, f32[256]{0:T(256)S(1)} %get-tuple-element.31, ...), kind=kCustom, calls=%fused_computation.44 | custom fusion | flops 2883584 | bytes 3674884 | tf_op jit(solution)/shard_map/scatter | solution.py:145
  98.5 2.4 convert_element_type.111
  101.0 1.4 convert_element_type.112
  102.4 32.3 %all_to_all.20 = bf16[32,12,1024]{2,1,0:T(8,128)(2,1)} all-to-all(bf16[32,12,1024]{2,1,0:T(8,128)(2,1)S(1)} %convert_element_type.112), channel_id=1, replica_groups=mesh['batch'=32,'node'=4,'replica'=2] {'batch'}, dimensions={0} | all-to-all | bytes 1572864 | tf_op jit(solution)/shard_map/all_to_all | solution.py:148
  134.7 2.4 reshape.377
  137.1 6.6 %scatter_custom_fusion.2 = f32[1024,1024]{1,0:T(8,128)} fusion(s32[384]{0:T(512)} %get-tuple-element.10, f32[384,1024]{1,0:T(8,128)} %reshape.377, f32[]{:T(128)} %constant.15.clone.1), kind=kCustom, calls=%fused_computation.11 | custom fusion | flops 393216 | bytes 4194816 | tf_op jit(solution)/shard_map/scatter-add | solution.py:159
  143.7 3.8 %convert_element_type.113 = bf16[1024,1024]{1,0:T(8,128)(2,1)} convert(f32[1024,1024]{1,0:T(8,128)} %scatter_custom_fusion.2) | non-fusion elementwise | flops 1048576 | bytes 6291456 | tf_op jit(solution)/shard_map/convert_element_type | solution.py:162
  147.6 4.0 %copy.52 = bf16[1024,1024]{0,1:T(8,128)(2,1)} copy(bf16[1024,1024]{1,0:T(8,128)(2,1)} %convert_element_type.113) | data formatting | bytes 4194304
  154.2 3.9 %fusion.19 = f32[16,4]{0,1:T(4,128)S(1)} fusion(f32[4,256,256]{2,0,1:T(4,128)} %copy.46, s32[256,256]{1,0:T(8,128)S(1)} %bitcast.117), kind=kOutput, calls=%fused_computation.39 | convolution fusion | flops 51380224 | bytes 1310976 | tf_op jit(solution)/shard_map/gijb,ghij->bh/dot_general | solution.py:111
  158.4 2.5 all-reduce.2
  160.8 72.1 %all-reduce = (f32[16,4]{0,1:T(4,128)S(1)}, f32[32,4]{0,1:T(4,128)S(1)}) all-reduce(f32[16,4]{0,1:T(4,128)S(1)} %get-tuple-element.17, f32[32,4]{0,1:T(4,128)S(1)} %get-tuple-element.18), channel_id=1, replica_groups=mesh['batch'=32,'node'=4,'replica'=2] {'batch'}, use_global_device_ids=true, to_apply=%region_23.24 | all-reduce | flops 192 | bytes 1536 | tf_op jit(solution)/shard_map/psum | solution.py:166
  236.1 82.3 %all-reduce.7.cloned.1.call-done = (f32[1024,256]{1,0:T(8,128)}, f32[1024,256]{1,0:T(8,128)}, f32[1024,256]{1,0:T(8,128)}, f32[256,1024]{1,0:T(8,128)}) async-done(((f32[1024,256]{1,0:T(8,128)}, f32[1024,256]{1,0:T(8,128)}, f32[1024,256]{1,0:T(8,128)}, f32[256,1024]{1,0:T(8,128)}), (f32[1024,256]{1,0:T(8,128)}, f32[1024,256]{1,0:T(8,128)}, f32[1024,256]{1,0:T(8,128)}, ...) | async-done | bytes 4194320 | tf_op jit(solution)/shard_map/psum | solution.py:166
  318.4 2.4 broadcast_multiply_fusion.3
  321.9 1.5 broadcast_multiply_fusion.1
  (93 shorter events, 20.7 us)
Async XLA Ops:
  8.0 27.6 %copy-start = (bf16[1024,1024]{1,0:T(8,128)(2,1)S(1)}, bf16[1024,1024]{1,0:T(8,128)(2,1)}, u32[]{:S(2)}) copy-start(bf16[1024,1024]{1,0:T(8,128)(2,1)} %param.13) | copy-start | bytes 6291460
  11.1 35.8 %copy-start.15 = (s32[256,1]{0,1:T(1,128)}, s32[256,1]{0,1:T(1,128)S(1)}, u32[]{:S(2)}) copy-start(s32[256,1]{0,1:T(1,128)S(1)} %compare_select_fusion.4) | copy-start | bytes 3076
  37.7 5.9 %copy-start.12 = (s32[1,256,256]{2,1,0:T(8,128)S(1)}, s32[1,256,256]{2,1,0:T(8,128)}, u32[]{:S(2)}) copy-start(s32[1,256,256]{2,1,0:T(8,128)} %param.17) | copy-start | bytes 786436
  37.7 5.9 %copy-start.16 = (f32[16,4]{0,1:T(4,128)S(1)}, f32[16,4]{0,1:T(4,128)}, u32[]{:S(2)}) copy-start(f32[16,4]{0,1:T(4,128)} %param.23) | copy-start | bytes 772
  38.9 32.2 %all-to-all-start.1 = ((bf16[32,12,1024]{2,1,0:T(8,128)(2,1)}), bf16[32,12,1024]{2,1,0:T(8,128)(2,1)}, u32[]{:S(2)}, u32[]{:S(2)}) async-start(bf16[32,12,1024]{2,1,0:T(8,128)(2,1)} %reshape.327), calls=%async_computation.1 | async-start | bytes 2097152 | tf_op jit(solution)/shard_map/all_to_all | solution.py:54
  43.5 3.4 %copy-start.17 = (f32[32,4]{0,1:T(4,128)S(1)}, f32[32,4]{0,1:T(4,128)}, u32[]{:S(2)}) copy-start(f32[32,4]{0,1:T(4,128)} %param.24) | copy-start | bytes 1540
  43.5 3.4 %copy-start.18 = (s32[1,256]{1,0:T(1,128)S(1)}, s32[1,256]{1,0:T(1,128)}, u32[]{:S(2)}) copy-start(s32[1,256]{1,0:T(1,128)} %param.18) | copy-start | bytes 3076
  43.5 108.1 %all-reduce.9.cloned.1.call-start = ((), (), s32[]{:S(2)}) async-start(), calls=%async_computation.6 | async-start | bytes 8388608 | tf_op jit(solution)/shard_map/psum | solution.py:166
  73.6 2.0 copy-start.11
  73.6 2.4 copy-start.3
  76.0 1.2 copy-start.9
  76.4 1.6 copy-start.4
  76.4 1.3 copy-start.20
  77.7 0.7 copy-start.21
  78.3 1.0 copy-start.1
  79.6 2.1 copy-start.22
  85.9 2.9 copy-start.5
  85.9 2.9 copy-start.14
  90.2 143.9 %reduce-scatter.4.cloned.1.call-start = ((), (), s32[]{:S(2)}) async-start(), calls=%async_computation.4 | async-start | bytes 2359296
  90.5 2.9 copy-start.10
  151.6 166.8 %all-reduce.7.cloned.1.call-start = ((), (), s32[]{:S(2)}) async-start(), calls=%async_computation.5 | async-start | bytes 8388608 | tf_op jit(solution)/shard_map/psum | solution.py:166
  151.6 1.2 copy-start.2
  152.9 1.3 copy-start.13
  152.9 5.3 %copy-start.19 = (s32[1,256]{1,0:T(1,128)S(1)}, s32[1,256]{1,0:T(1,128)}, u32[]{:S(2)}) copy-start(s32[1,256]{1,0:T(1,128)} %param.18) | copy-start | bytes 3076
  318.4 2.4 copy-start.6
  318.4 3.5 %copy-start.7 = (f32[1024,256]{1,0:T(8,128)S(1)}, f32[1024,256]{1,0:T(8,128)}, u32[]{:S(2)}) copy-start(f32[1024,256]{1,0:T(8,128)} %get-tuple-element.14) | copy-start | bytes 3145732
  318.4 3.5 %copy-start.8 = (f32[1024,256]{1,0:T(8,128)S(1)}, f32[1024,256]{1,0:T(8,128)}, u32[]{:S(2)}) copy-start(f32[1024,256]{1,0:T(8,128)} %get-tuple-element.15) | copy-start | bytes 3145732
Sparse Core Ops, SparseCore 0:
  90.3 36.0 all-reduce.8
  156.9 161.4 all-reduce.6
Sparse Core Ops, SparseCore 1:
  151.6 29.6 reduce-scatter.3
